TPU v7x, 32 devices: a whole 2x2x4 slice. The times are simulated.
32 devices in a mesh: dp: 4 (over y, x), ctx: 4 (over z), tp: 2 (over core).
Axes of the slice: x: 2, y: 2, z: 4, core: 2. Of those that a mesh axis runs over, the one named last changes fastest.
Arguments:
- cotangent: bfloat16 [6144, 4096], P(('dp', 'ctx')), may hold values from -6 to 6
- gate_pre: bfloat16 [6144, 16384], P(('dp', 'ctx'), 'tp'), may hold values from -6 to 6
- up_pre: bfloat16 [6144, 16384], P(('dp', 'ctx'), 'tp'), may hold values from -6 to 6
- w_down: bfloat16 [4096, 16384], P(('dp', 'ctx'), 'tp'), may hold values from -0.046875 to 0.046875
Outputs:
- grad_gate: bfloat16 [6144, 16384], P(('dp', 'ctx'), 'tp')
- grad_up: bfloat16 [6144, 16384], P(('dp', 'ctx'), 'tp')
- grad_down: bfloat16 [4096, 16384], P(('dp', 'ctx'), 'tp')
All inputs are finite; a program needn't handle non-finite values.
Results may differ from a plain program's by a relative error of at most 0.018.
Values may be sent and summed in bfloat16 or wider, within the bound.
A program may use at most 192 MiB of HBM per device.

v0:
```python
import jax
import jax.numpy as jnp
from jax import lax
from jax.sharding import PartitionSpec as P


def local(cotangent, gate_pre, up_pre, w_down):
    gate_wide = gate_pre.astype(jnp.float32)
    up_wide = up_pre.astype(jnp.float32)
    sigmoid_gate = jax.nn.sigmoid(gate_wide)
    activated = gate_wide * sigmoid_gate
    hidden = (activated * up_wide).astype(jnp.bfloat16)
    groups = lax.axis_size(("dp", "ctx"))
    group_rows = cotangent.shape[0]
    hidden_width = hidden.shape[1]
    owned_rows = w_down.shape[0]
    grad_hidden = jnp.dot(
        cotangent,
        lax.all_gather(w_down, ("dp", "ctx"), axis=0, tiled=True),
        preferred_element_type=jnp.float32,
    )
    grad_gate = (
        grad_hidden * up_wide * sigmoid_gate * (1.0 + gate_wide * (1.0 - sigmoid_gate))
    ).astype(jnp.bfloat16)
    grad_up = (grad_hidden * activated).astype(jnp.bfloat16)
    grad_gate, grad_up = (grad_gate, grad_up)
    every_hidden = lax.all_gather(hidden, ("dp", "ctx"), axis=0, tiled=True)
    owned_columns = lax.all_to_all(
        cotangent, ("dp", "ctx"), split_axis=1, concat_axis=0, tiled=True
    )
    hid_groups = every_hidden.reshape(groups, group_rows, hidden_width)
    cot_groups = owned_columns.reshape(groups, group_rows, owned_rows)
    partial_value = jnp.einsum(
        "gri,grf->gif", cot_groups, hid_groups, preferred_element_type=jnp.float32
    ).astype(jnp.bfloat16)
    summed = jnp.sum(partial_value.astype(jnp.float32), axis=0)
    grad_down = (summed / groups).astype(jnp.bfloat16)
    return (grad_gate, grad_up, grad_down)


def solution(mesh):
    in_specs = (
        P(("dp", "ctx"), None),
        P(("dp", "ctx"), "tp"),
        P(("dp", "ctx"), "tp"),
        P(("dp", "ctx"), "tp"),
    )
    out_specs = (P(("dp", "ctx"), "tp"), P(("dp", "ctx"), "tp"), P(("dp", "ctx"), "tp"))
    return jax.shard_map(local, mesh=mesh, in_specs=in_specs, out_specs=out_specs, check_vma=False)
```

profile of v0, /device:TPU:0, one launch (start us, length us, event | category | flops | bytes accessed | tf_op | source)
XLA Modules:
  0.0 1845.5 jit_solution(15286276973045502541)
XLA Ops:
  7.2 0.0 all-gather.3.cloned.1.call-start
  7.2 0.7 all-gather.3.cloned.1.call-update
  7.9 0.0 all-gather.5.cloned.1.call-start
  7.9 674.3 %all-gather.3.cloned.1.call-done = bf16[4096,8192]{1,0:T(8,128)(2,1)} async-done(((bf16[256,8192]{1,0:T(8,128)(2,1)}), bf16[4096,8192]{1,0:T(8,128)(2,1)}) %all-gather.3.cloned.1.call-update) | async-done | bytes 67108880 | tf_op jit(solution)/shard_map/all_gather | solution.py:19
  682.3 42.0 %multiply_convert_fusion = (bf16[384,8192]{1,0:T(8,128)(2,1)}, bf16[384,8192]{1,0:T(8,128)(2,1)}, bf16[384,8192]{1,0:T(8,128)(2,1)}) fusion(bf16[384,8192]{1,0:T(8,128)(2,1)} %param.5, bf16[384,8192]{1,0:T(8,128)(2,1)} %param.6, bf16[384,4096]{1,0:T(8,128)(2,1)} %param.4, bf16[4096,8192]{1,0:T(8,128)(2,1)} %all-gather.3.cloned.1.call-done), kind=kOutput, calls=%fused_computation.14 | convolution fusion | flops 25823281152 | bytes 101711872 | tf_op jit(solution)/shard_map/dot_general | solution.py:17
  724.3 0.0 copy-start
  724.3 0.0 all-gather.5.cloned.1.call-update
  724.3 1.9 copy-done
  726.1 2.8 copy.11
  728.9 3.6 copy.12
  732.6 159.7 %all_to_all.16 = bf16[384,16,256]{2,0,1:T(8,128)(2,1)} all-to-all(bf16[384,16,256]{2,0,1:T(8,128)(2,1)S(1)} %copy.12), channel_id=1, replica_groups=mesh['dp'=4,'ctx'=4,'tp'=2] {'dp','ctx'}, dimensions={1} | all-to-all | bytes 6291456 | tf_op jit(solution)/shard_map/all_to_all | solution.py:28
  892.3 879.3 %all-gather.5.cloned.1.call-done = bf16[6144,8192]{1,0:T(8,128)(2,1)} async-done(((bf16[384,8192]{1,0:T(8,128)(2,1)}), bf16[6144,8192]{1,0:T(8,128)(2,1)}) %all-gather.5.cloned.1.call-update) | async-done | bytes 100663312 | tf_op jit(solution)/shard_map/all_gather | solution.py:27
  1771.6 54.7 %convert_reduce_fusion = f32[8192,256]{1,0:T(8,128)} fusion(bf16[16,384,8192]{2,1,0:T(8,128)(2,1)} %bitcast, bf16[384,16,256]{2,0,1:T(8,128)(2,1)} %all_to_all.16), kind=kOutput, calls=%fused_computation | convolution fusion | flops 25868369920 | bytes 112197632 | tf_op jit(solution)/shard_map/gri,grf->gif/dot_general | solution.py:33
  1826.3 6.0 fusion.8
  1832.3 6.3 copy.14
Async XLA Ops:
  7.2 675.1 %all-gather.3.cloned.1.call-start = ((), (), s32[]{:S(2)}) async-start(), calls=%async_computation.1 | async-start | bytes 71303168 | tf_op jit(solution)/shard_map/all_gather | solution.py:19
  7.9 1763.7 %all-gather.5.cloned.1.call-start = ((), (), s32[]{:S(2)}) async-start(), calls=%async_computation.2 | async-start | bytes 106954752 | tf_op jit(solution)/shard_map/all_gather | solution.py:27
  724.3 1.9 copy-start
Sparse Core Ops, SparseCore 0:
  10.8 671.4 all-gather.2
  724.4 1047.1 all-gather.4
where the time goes:
time: 1850 us
  waiting for transfers between devices  1550 us (84%)
  blocking collectives  160 us (9%)
  matrix products  96.7 us (5%)
    all_gather x1, waiting for transfers between devices, local(): every_hidden = lax.all_gather(hidden, ('dp', 'ctx'), axis=0, tiled=True)  879 us
    all_gather x1, waiting for transfers between devices, local(): lax.all_gather(w_down, ('dp', 'ctx'), axis=0, tiled=True)  674 us
    all_to_all x1, blocking collectives, local(): lax.all_to_all(cotangent, ('dp', 'ctx'), split_axis=1, concat_axis=0, til...  160 us
    dot_general x1, matrix products, local(): jnp.einsum('gri,grf->gif', cot_groups, hid_groups, preferred_element_type...  54.7 us
    dot_general x1, matrix products, local(): jnp.dot(cotangent, lax.all_gather(w_down, ('dp', 'ctx'), axis=0, tiled=Tr...  42 us
  transfers between devices with their start and end apart: 2, of which 2 were waited for; matrix products, arithmetic and copies ran while one was open for 0% of the time, Pallas kernels for 0%

commit v1 on v0

v1 whole, which is shorter than its diff:
```python
import jax
import jax.numpy as jnp
from jax import lax
from jax.sharding import PartitionSpec as P

together = lax.optimization_barrier


def swap(value, distance):
    pairs = [(at, at ^ distance) for at in range(lax.axis_size("dp"))]
    return lax.ppermute(value, "dp", pairs)


def wide(value):
    return value.astype(jnp.float32)


class Gather:
    def __init__(self, value):
        self.own, self.up, self.down = value, [value], [value]

    def step(self):
        size, step = lax.axis_size("ctx"), len(self.up)
        up = lax.ppermute(self.up[-1], "ctx", [(k, k + 1) for k in range(step - 1, size - 1)])
        down = lax.ppermute(self.down[-1], "ctx", [(k, k - 1) for k in range(1, size - step + 1)])
        return [up, down]

    def keep(self, arrived):
        self.up.append(arrived[0])
        self.down.append(arrived[1])

    def whole(self):
        size, at = lax.axis_size("ctx"), lax.axis_index("ctx")
        return jnp.concatenate(
            [self.own]
            + [jnp.where(at >= j, self.up[j], self.down[size - j]) for j in range(1, size)]
        )


class Scatter:
    def __init__(self, partial):
        self.partial, self.arrived, self.count = partial, None, 0

    def block(self, target):
        size = lax.axis_size("ctx")
        rows = self.partial.shape[0] // size
        start = jnp.clip(target, 0, size - 1) * rows
        return lax.dynamic_slice_in_dim(self.partial, start, rows, 0)

    def step(self):
        size, at = lax.axis_size("ctx"), lax.axis_index("ctx")
        self.count += 1
        step = self.count
        up, down = self.block(at + size - step), self.block(at - size + step)
        if step > 1:
            up, down = up + self.arrived[0], down + self.arrived[1]
        return [
            lax.ppermute(up, "ctx", [(k, k + 1) for k in range(step)]),
            lax.ppermute(down, "ctx", [(size - 1 - k, size - 2 - k) for k in range(step)]),
        ]

    def keep(self, arrived):
        self.arrived = arrived

    def total(self):
        return (
            wide(self.block(lax.axis_index("ctx")))
            + wide(self.arrived[0])
            + wide(self.arrived[1])
        )


def send_first(partial):
    rows = partial.shape[0] // 4
    half = rows // 2
    for_x, for_y, across = [partial[k * rows : (k + 1) * rows] for k in (1, 2, 3)]
    return [
        swap(across[:half], 1),
        swap(across[half:], 2),
        swap(for_x[:half], 1),
        swap(for_y[half:], 2),
    ]


def send_second(partial, first):
    rows = partial.shape[0] // 4
    half = rows // 2
    return [
        swap(partial[rows + half : 2 * rows] + first[1], 1),
        swap(partial[2 * rows : 2 * rows + half] + first[0], 2),
    ]


def sum_plane(partial, first, second):
    rows = partial.shape[0] // 4
    half = rows // 2
    return jnp.concatenate(
        [
            wide(partial[:half]) + wide(first[2]) + wide(second[1]),
            wide(partial[half:rows]) + wide(second[0]) + wide(first[3]),
        ]
    )


def local(cotangent, gate_pre, up_pre, w_down):
    groups = lax.axis_size(("dp", "ctx"))
    size, at = lax.axis_size("ctx"), lax.axis_index("ctx")
    width = gate_pre.shape[1] // 2
    owned = cotangent.shape[1] // lax.axis_size("dp")
    small = owned // size
    half = cotangent.shape[0] // 2
    me = lax.axis_index("dp")
    cuts = (slice(0, width), slice(width, 2 * width))

    def features(k):
        return lax.dynamic_slice_in_dim(cotangent, (me ^ k) * owned, owned, 1)

    def activation(cut):
        gate = wide(gate_pre[:, cut])
        return (gate * jax.nn.sigmoid(gate) * wide(up_pre[:, cut])).astype(jnp.bfloat16)

    def weight_dot(gathered):
        return jnp.dot(turned, gathered.whole(), preferred_element_type=jnp.float32).astype(
            jnp.bfloat16
        )

    def down_dot(parts):
        return lax.dot_general(
            block,
            jnp.concatenate(parts),
            (((0,), (0,)), ((), ())),
            preferred_element_type=jnp.float32,
        ).astype(jnp.bfloat16)

    def finish(cut, grad_hidden):
        gate, up = wide(gate_pre[:, cut]), wide(up_pre[:, cut])
        s = jax.nn.sigmoid(gate)
        return (
            (grad_hidden * up * s * (1.0 + gate * (1.0 - s))).astype(jnp.bfloat16),
            (grad_hidden * (gate * s)).astype(jnp.bfloat16),
        )

    g0, g1 = Gather(w_down[:, cuts[0]]), Gather(w_down[:, cuts[1]])
    h0 = activation(cuts[0])
    a, b, c, x0, h1 = together(
        (
            g0.step(),
            g1.step(),
            [features(0)] + [swap(features(k), k) for k in (1, 2, 3)],
            [swap(h0, 1), swap(h0, 2)],
            activation(cuts[1]),
        )
    )
    g0.keep(a)
    g1.keep(b)
    block = jnp.concatenate(c)
    turned = jnp.concatenate(
        [
            lax.dynamic_slice_in_dim(block, lax.rem(at - j + size, size) * small, small, 1)
            for j in range(size)
        ],
        axis=1,
    )
    a, b, y0, x1 = together(
        (
            g0.step(),
            g1.step(),
            [swap(x0[1][:half], 1), swap(x0[0][half:], 2)],
            [swap(h1, 1), swap(h1, 2)],
        )
    )
    g0.keep(a)
    g1.keep(b)
    a, y1, d0 = together(
        (
            g0.step(),
            [swap(x1[1][:half], 1), swap(x1[0][half:], 2)],
            down_dot([h0] + x0 + y0),
        )
    )
    g0.keep(a)
    s0 = Scatter(d0)
    a, b, p0, d1 = together(
        (s0.step(), g1.step(), weight_dot(g0), down_dot([h1] + x1 + y1))
    )
    s0.keep(a)
    g1.keep(b)
    s1 = Scatter(d1)
    a, b, f0, p1 = together((s0.step(), s1.step(), send_first(p0), weight_dot(g1)))
    s0.keep(a)
    s1.keep(b)
    a, b, e0, f1 = together((s0.step(), s1.step(), send_second(p0, f0), send_first(p1)))
    s0.keep(a)
    s1.keep(b)
    a, e1, o0 = together(
        (s1.step(), send_second(p1, f1), finish(cuts[0], sum_plane(p0, f0, e0)))
    )
    s1.keep(a)
    o1 = finish(cuts[1], sum_plane(p1, f1, e1))
    down = [(s.total() / groups).astype(jnp.bfloat16) for s in (s0, s1)]
    return (
        jnp.concatenate([o0[0], o1[0]], axis=1),
        jnp.concatenate([o0[1], o1[1]], axis=1),
        jnp.concatenate(down, axis=1),
    )


def solution(mesh):
    in_specs = (
        P(("dp", "ctx"), None),
        P(("dp", "ctx"), "tp"),
        P(("dp", "ctx"), "tp"),
        P(("dp", "ctx"), "tp"),
    )
    out_specs = (P(("dp", "ctx"), "tp"), P(("dp", "ctx"), "tp"), P(("dp", "ctx"), "tp"))
    return jax.shard_map(local, mesh=mesh, in_specs=in_specs, out_specs=out_specs, check_vma=False)
```

time: 1850 us -> 759 us (0.41)
  waiting for transfers between devices: 1550 us -> 435 us
  blocking collectives: 160 us -> 0 us
  starting transfers between devices: 0.08 us -> 88.9 us
  other arithmetic: 6.04 us -> 92.5 us
  local copies, waits for them, and re-layouts: 14.6 us -> 61.7 us
  matrix products: 96.7 us -> 71.9 us
    all_gather x2 -> x0, waiting for transfers between devices: 1550 us -> none  [the longest x1 879 us: local(): every_hidden = lax.all_gather(hidden, ('dp', 'ctx'), axis=0, tiled=True)]
    ppermute x0 -> x47, waiting for transfers between devices: none -> 435 us  [the longest x23 249 us: swap(): return lax.ppermute(value, 'dp', pairs)]
    all_to_all x1 -> x0, blocking collectives: 160 us -> none  [local(): lax.all_to_all(cotangent, ('dp', 'ctx'), split_axis=1, concat_axis=0, til...]
    ppermute x0 -> x47, starting transfers between devices: none -> 88.9 us  [the longest x6 28.8 us: step(): lax.ppermute(up, 'ctx', [(k, k + 1) for k in range(step)])]
    add x0 -> x8, other arithmetic: none -> 45.5 us  [the longest x4 24.4 us: step(): up, down = (up + self.arrived[0], down + self.arrived[1])]
    dot_general x2 -> x4, matrix products: 96.7 us -> 71.9 us  [the longest x2 38.4 us: weight_dot(): jnp.dot(turned, gathered.whole(), preferred_element_type=jnp.float32)]
    slice x0 -> x7, local copies, waits for them, and re-layouts: none -> 24.3 us  [the longest x2 13.2 us: send_first(): for_y[half:]]
  transfers between devices with their start and end apart: 2 -> 47, of which waited for: 2 -> 20; matrix products, arithmetic and copies ran while one was open for 0% -> 22% of each run, Pallas kernels for 0% -> 0%
where the time goes in v1:
time: 759 us; the launch traced here: 752 us
  waiting for transfers between devices  435 us (57%)
  other arithmetic  92.5 us (12%)
  starting transfers between devices  88.9 us (12%)
  matrix products  71.9 us (9%)
  local copies, waits for them, and re-layouts  61.7 us (8%)
    ppermute x23, waiting for transfers between devices, swap(): return lax.ppermute(value, 'dp', pairs)  249 us
    ppermute x6, waiting for transfers between devices, step(): lax.ppermute(self.down[-1], 'ctx', [(k, k - 1) for k in range(1, size - s...  158 us
    dot_general x2, matrix products, weight_dot(): jnp.dot(turned, gathered.whole(), preferred_element_type=jnp.float32)  38.4 us
    dot_general x2, matrix products, down_dot(): lax.dot_general(block, jnp.concatenate(parts), (((0,), (0,)), ((), ())),...  33.5 us
    ppermute x6, starting transfers between devices, step(): lax.ppermute(up, 'ctx', [(k, k + 1) for k in range(step)])  28.8 us
    ppermute x23, starting transfers between devices, swap(): return lax.ppermute(value, 'dp', pairs)  24.8 us
    add x4, other arithmetic, step(): up, down = (up + self.arrived[0], down + self.arrived[1])  24.4 us
    unnamed x86, local copies, waits for them, and re-layouts  21.8 us
  transfers between devices with their start and end apart: 47, of which 20 were waited for; matrix products, arithmetic and copies ran while one was open for 22% of the time, Pallas kernels for 0%

profile of v1, /device:TPU:0, one launch (start us, length us, event | category | flops | bytes accessed | tf_op | source)
XLA Modules:
  0.0 751.8 jit_solution(2220924550559681333)
XLA Ops:
  28.3 93.1 %collective-permute-done.5 = bf16[384,1024]{1,0:T(8,128)(2,1)S(1)} collective-permute-done((bf16[384,1024]{1,0:T(8,128)(2,1)S(1)}, bf16[384,1024]{1,0:T(8,128)(2,1)S(1)}, u32[]{:S(2)}, u32[]{:S(2)}) %collective-permute-start.5) | collective-permute-done | bytes 786464 | tf_op jit(solution)/shard_map/ppermute | solution.py:11
  131.7 40.3 %collective-permute-done.1 = bf16[256,4096]{1,0:T(8,128)(2,1)} collective-permute-done((bf16[256,4096]{1,0:T(8,128)(2,1)S(1)}, bf16[256,4096]{1,0:T(8,128)(2,1)}, u32[]{:S(2)}, u32[]{:S(2)}) %collective-permute-start.1) | collective-permute-done | bytes 2097184 | tf_op jit(solution)/shard_map/ppermute | solution.py:25
  171.9 41.9 %collective-permute-done.3 = bf16[256,4096]{1,0:T(8,128)(2,1)S(1)} collective-permute-done((bf16[256,4096]{1,0:T(8,128)(2,1)S(1)}, bf16[256,4096]{1,0:T(8,128)(2,1)S(1)}, u32[]{:S(2)}, u32[]{:S(2)}) %collective-permute-start.3) | collective-permute-done | bytes 2097184 | tf_op jit(solution)/shard_map/ppermute | solution.py:25
  224.7 29.8 %collective-permute-done.13 = bf16[192,4096]{1,0:T(8,128)(2,1)} collective-permute-done((bf16[192,4096]{1,0:T(8,128)(2,1)}, bf16[192,4096]{1,0:T(8,128)(2,1)}, u32[]{:S(2)}, u32[]{:S(2)}) %collective-permute-start.13) | collective-permute-done | bytes 1572896 | tf_op jit(solution)/shard_map/ppermute | solution.py:11
  274.7 31.0 %collective-permute-done.12 = bf16[256,4096]{1,0:T(8,128)(2,1)} collective-permute-done((bf16[256,4096]{1,0:T(8,128)(2,1)}, bf16[256,4096]{1,0:T(8,128)(2,1)}, u32[]{:S(2)}, u32[]{:S(2)}) %collective-permute-start.12) | collective-permute-done | bytes 2097184 | tf_op jit(solution)/shard_map/ppermute | solution.py:25
  305.7 12.3 %collective-permute-done.15 = bf16[384,4096]{1,0:T(8,128)(2,1)} collective-permute-done((bf16[384,4096]{1,0:T(8,128)(2,1)S(1)}, bf16[384,4096]{1,0:T(8,128)(2,1)}, u32[]{:S(2)}, u32[]{:S(2)}) %collective-permute-start.15) | collective-permute-done | bytes 3145760 | tf_op jit(solution)/shard_map/ppermute | solution.py:11
  347.3 16.6 %convolution_convert_fusion.3 = bf16[1024,4096]{1,0:T(8,128)(2,1)S(1)} fusion(bf16[1536,1024]{1,0:T(8,128)(2,1)S(1)} %constant_dynamic-update-slice_fusion, bf16[1536,4096]{1,0:T(8,128)(2,1)} %constant_dynamic-update-slice_fusion.4), kind=kOutput, calls=%fused_computation.27 | convolution fusion | flops 12889096192 | bytes 24117248 | tf_op jit(solution)/shard_map/dot_general | solution.py:128
  365.3 39.1 %collective-permute-done.18 = bf16[256,4096]{1,0:T(8,128)(2,1)S(1)} collective-permute-done((bf16[256,4096]{1,0:T(8,128)(2,1)}, bf16[256,4096]{1,0:T(8,128)(2,1)S(1)}, u32[]{:S(2)}, u32[]{:S(2)}) %collective-permute-start.18) | collective-permute-done | bytes 2097184 | tf_op jit(solution)/shard_map/ppermute | solution.py:25
  416.9 19.3 %convolution_convert_fusion.1 = bf16[1536,4096]{1,0:T(8,128)(2,1)} fusion(bf16[256,4096]{1,0:T(8,128)(2,1)} %broadcast_select_fusion.1, bf16[256,4096]{1,0:T(8,128)(2,1)} %broadcast_select_fusion.3, bf16[256,4096]{1,0:T(8,128)(2,1)} %broadcast_select_fusion.5, bf16[256,4096]{1,0:T(8,128)(2,1)} %copy-done.16, bf16[1536,256]{1,0:T(8,128)(2,1)} %get-tuple-element.150, ...), kind=kOutput, calls=%fused_computation.1 | convolution fusion | flops 12937330688 | bytes 24117248 | tf_op jit(solution)/shard_map/dot_general | solution.py:123
  441.9 16.9 %convolution_convert_fusion.2 = bf16[1024,4096]{1,0:T(8,128)(2,1)S(1)} fusion(bf16[1536,1024]{1,0:T(8,128)(2,1)S(1)} %copy-done.9, bf16[1536,4096]{1,0:T(8,128)(2,1)} %constant_dynamic-update-slice_fusion.9), kind=kOutput, calls=%fused_computation.26 | convolution fusion | flops 12889096192 | bytes 24117248 | tf_op jit(solution)/shard_map/dot_general | solution.py:128
  458.9 8.1 %fusion.34 = (bf16[192,4096]{1,0:T(8,128)(2,1)}, bf16[192,4096]{1,0:T(8,128)(2,1)S(1)}, bf16[192,4096]{1,0:T(8,128)(2,1)S(1)}, bf16[192,4096]{1,0:T(8,128)(2,1)}) fusion(bf16[1536,4096]{1,0:T(8,128)(2,1)} %convolution_convert_fusion.1), kind=kLoop, calls=%fused_computation.105 | loop fusion | bytes 12582912 | tf_op jit(solution)/shard_map/slice | solution.py:81
  486.4 13.7 %collective-permute-done.29 = bf16[192,4096]{1,0:T(8,128)(2,1)} collective-permute-done((bf16[192,4096]{1,0:T(8,128)(2,1)}, bf16[192,4096]{1,0:T(8,128)(2,1)}, u32[]{:S(2)}, u32[]{:S(2)}) %collective-permute-start.29) | collective-permute-done | bytes 1572896 | tf_op jit(solution)/shard_map/ppermute | solution.py:11
  505.3 11.7 %collective-permute-done.31 = bf16[192,4096]{1,0:T(8,128)(2,1)} collective-permute-done((bf16[192,4096]{1,0:T(8,128)(2,1)S(1)}, bf16[192,4096]{1,0:T(8,128)(2,1)}, u32[]{:S(2)}, u32[]{:S(2)}) %collective-permute-start.31) | collective-permute-done | bytes 1572896 | tf_op jit(solution)/shard_map/ppermute | solution.py:11
  519.0 19.2 %convolution_convert_fusion = bf16[1536,4096]{1,0:T(8,128)(2,1)} fusion(bf16[256,4096]{1,0:T(8,128)(2,1)} %get-tuple-element.157, bf16[256,4096]{1,0:T(8,128)(2,1)S(1)} %broadcast_select_fusion.2, bf16[256,4096]{1,0:T(8,128)(2,1)} %get-tuple-element.158, bf16[256,4096]{1,0:T(8,128)(2,1)} %copy-done.15, bf16[1536,256]{1,0:T(8,128)(2,1)} %get-tuple-element.150, ...), kind=kOutput, calls=%fused_computation | convolution fusion | flops 12937330688 | bytes 24117248 | tf_op jit(solution)/shard_map/dot_general | solution.py:123
  538.2 6.2 collective-permute-done.25
  569.6 15.5 %collective-permute-done.37 = bf16[192,4096]{1,0:T(8,128)(2,1)S(1)} collective-permute-done((bf16[192,4096]{1,0:T(8,128)(2,1)S(1)}, bf16[192,4096]{1,0:T(8,128)(2,1)S(1)}, u32[]{:S(2)}, u32[]{:S(2)}) %collective-permute-start.37) | collective-permute-done | bytes 1572896 | tf_op jit(solution)/shard_map/ppermute | solution.py:11
  592.8 19.8 %collective-permute-done.39 = bf16[192,4096]{1,0:T(8,128)(2,1)} collective-permute-done((bf16[192,4096]{1,0:T(8,128)(2,1)S(1)}, bf16[192,4096]{1,0:T(8,128)(2,1)}, u32[]{:S(2)}, u32[]{:S(2)}) %collective-permute-start.39) | collective-permute-done | bytes 1572896 | tf_op jit(solution)/shard_map/ppermute | solution.py:11
  620.1 9.4 %collective-permute-done.41 = bf16[192,4096]{1,0:T(8,128)(2,1)} collective-permute-done((bf16[192,4096]{1,0:T(8,128)(2,1)S(1)}, bf16[192,4096]{1,0:T(8,128)(2,1)}, u32[]{:S(2)}, u32[]{:S(2)}) %collective-permute-start.41) | collective-permute-done | bytes 1572896 | tf_op jit(solution)/shard_map/ppermute | solution.py:11
  629.9 35.8 %collective-permute-done.42 = bf16[192,4096]{1,0:T(8,128)(2,1)} collective-permute-done((bf16[192,4096]{1,0:T(8,128)(2,1)}, bf16[192,4096]{1,0:T(8,128)(2,1)}, u32[]{:S(2)}, u32[]{:S(2)}) %collective-permute-start.42) | collective-permute-done | bytes 1572896 | tf_op jit(solution)/shard_map/ppermute | solution.py:11
  671.5 6.6 dynamic-slice_add_fusion
  678.1 9.1 %collective-permute-start.43 = (bf16[256,4096]{1,0:T(8,128)(2,1)}, bf16[256,4096]{1,0:T(8,128)(2,1)}, u32[]{:S(2)}, u32[]{:S(2)}) collective-permute-start(bf16[256,4096]{1,0:T(8,128)(2,1)} %get-tuple-element.136), channel_id=1, source_target_pairs={{0,2},{2,4},{4,6},{1,3},{3,5},{5,7},{8,10},{10,12},{12,14},{9,11},... | collective-permute-start | bytes 6291464 | tf_op jit(solution)/shard_map/ppermute | solution.py:58
  703.1 6.6 collective-permute-done.43
  709.7 15.1 %collective-permute-done.44 = bf16[256,4096]{1,0:T(8,128)(2,1)} collective-permute-done((bf16[256,4096]{1,0:T(8,128)(2,1)}, bf16[256,4096]{1,0:T(8,128)(2,1)}, u32[]{:S(2)}, u32[]{:S(2)}) %collective-permute-start.44) | collective-permute-done | bytes 2097184 | tf_op jit(solution)/shard_map/ppermute | solution.py:59
  731.4 8.1 %convert_add_fusion.1 = (f32[192,4096]{1,0:T(8,128)}, f32[192,4096]{1,0:T(8,128)}) fusion(bf16[192,4096]{1,0:T(8,128)(2,1)} %collective-permute-done.46, bf16[192,4096]{1,0:T(8,128)(2,1)} %collective-permute-done.41, bf16[1536,4096]{1,0:T(8,128)(2,1)} %convolution_convert_fusion, bf16[192,4096]{1,0:T(8,128)(2,1)} %collective-permute-done.42, ...), kind=kLoop, calls=%fused_computation.55 | loop fusion | flops 7864320 | bytes 15728640 | tf_op jit(solution)/shard_map/add | solution.py:99
  (202 shorter events, 225.0 us)
Async XLA Ops:
  9.6 118.7 %collective-permute-start = (bf16[256,4096]{1,0:T(8,128)(2,1)S(1)}, bf16[256,4096]{1,0:T(8,128)(2,1)}, u32[]{:S(2)}, u32[]{:S(2)}) collective-permute-start(bf16[256,4096]{1,0:T(8,128)(2,1)S(1)} %get-tuple-element.148), channel_id=1, source_target_pairs={{0,2},{2,4},{4,6},{1,3},{3,5},{5,7},{8,10},{10,12},{12,14},{9,11},... | collective-permute-start | bytes 6291464 | tf_op jit(solution)/shard_map/ppermute | solution.py:24
  18.3 195.5 %collective-permute-start.7 = (bf16[384,4096]{1,0:T(8,128)(2,1)S(1)}, bf16[384,4096]{1,0:T(8,128)(2,1)S(1)}, u32[]{:S(2)}, u32[]{:S(2)}) collective-permute-start(bf16[384,4096]{1,0:T(8,128)(2,1)S(1)} %get-tuple-element.114), channel_id=1, source_target_pairs={{0,8},{8,0},{16,24},{24,16},{1,9},{9,1},{17,25},{25,17},{2,10},{10... | collective-permute-start | bytes 9437192 | tf_op jit(solution)/shard_map/ppermute | solution.py:11
  18.6 195.2 %collective-permute-start.8 = (bf16[384,4096]{1,0:T(8,128)(2,1)S(1)}, bf16[384,4096]{1,0:T(8,128)(2,1)S(1)}, u32[]{:S(2)}, u32[]{:S(2)}) collective-permute-start(bf16[384,4096]{1,0:T(8,128)(2,1)S(1)} %get-tuple-element.114), channel_id=1, source_target_pairs={{0,16},{8,24},{16,0},{24,8},{1,17},{9,25},{17,1},{25,9},{2,18},{10... | collective-permute-start | bytes 9437192 | tf_op jit(solution)/shard_map/ppermute | solution.py:11
  20.1 101.2 %collective-permute-start.5 = (bf16[384,1024]{1,0:T(8,128)(2,1)S(1)}, bf16[384,1024]{1,0:T(8,128)(2,1)S(1)}, u32[]{:S(2)}, u32[]{:S(2)}) collective-permute-start(bf16[384,1024]{1,0:T(8,128)(2,1)S(1)} %get-tuple-element.156), channel_id=1, source_target_pairs={{0,16},{8,24},{16,0},{24,8},{1,17},{9,25},{17,1},{25,9},{2,18},{10... | collective-permute-start | bytes 2359304 | tf_op jit(solution)/shard_map/ppermute | solution.py:11
  25.2 97.4 %collective-permute-start.6 = (bf16[384,1024]{1,0:T(8,128)(2,1)S(1)}, bf16[384,1024]{1,0:T(8,128)(2,1)S(1)}, u32[]{:S(2)}, u32[]{:S(2)}) collective-permute-start(bf16[384,1024]{1,0:T(8,128)(2,1)S(1)} %get-tuple-element.153), channel_id=1, source_target_pairs={{0,24},{8,16},{16,8},{24,0},{1,25},{9,17},{17,9},{25,1},{2,26},{10... | collective-permute-start | bytes 2359304 | tf_op jit(solution)/shard_map/ppermute | solution.py:11
  121.4 50.6 %collective-permute-start.1 = (bf16[256,4096]{1,0:T(8,128)(2,1)S(1)}, bf16[256,4096]{1,0:T(8,128)(2,1)}, u32[]{:S(2)}, u32[]{:S(2)}) collective-permute-start(bf16[256,4096]{1,0:T(8,128)(2,1)S(1)} %get-tuple-element.148), channel_id=1, source_target_pairs={{2,0},{4,2},{6,4},{3,1},{5,3},{7,5},{10,8},{12,10},{14,12},{11,9},... | collective-permute-start | bytes 6291464 | tf_op jit(solution)/shard_map/ppermute | solution.py:25
  128.3 85.5 %collective-permute-start.3 = (bf16[256,4096]{1,0:T(8,128)(2,1)S(1)}, bf16[256,4096]{1,0:T(8,128)(2,1)S(1)}, u32[]{:S(2)}, u32[]{:S(2)}) collective-permute-start(bf16[256,4096]{1,0:T(8,128)(2,1)S(1)} %get-tuple-element.147), channel_id=1, source_target_pairs={{2,0},{4,2},{6,4},{3,1},{5,3},{7,5},{10,8},{12,10},{14,12},{11,9},... | collective-permute-start | bytes 6291464 | tf_op jit(solution)/shard_map/ppermute | solution.py:25
  213.8 50.8 %collective-permute-start.10 = (bf16[256,4096]{1,0:T(8,128)(2,1)}, bf16[256,4096]{1,0:T(8,128)(2,1)}, u32[]{:S(2)}, u32[]{:S(2)}) collective-permute-start(bf16[256,4096]{1,0:T(8,128)(2,1)} %collective-permute-done.1), channel_id=1, source_target_pairs={{2,0},{4,2},{3,1},{5,3},{10,8},{12,10},{11,9},{13,11},{18,16},{20,... | collective-permute-start | bytes 6291464 | tf_op jit(solution)/shard_map/ppermute | solution.py:25
  221.1 96.9 %collective-permute-start.15 = (bf16[384,4096]{1,0:T(8,128)(2,1)S(1)}, bf16[384,4096]{1,0:T(8,128)(2,1)}, u32[]{:S(2)}, u32[]{:S(2)}) collective-permute-start(bf16[384,4096]{1,0:T(8,128)(2,1)S(1)} %fusion.18), channel_id=1, source_target_pairs={{0,8},{8,0},{16,24},{24,16},{1,9},{9,1},{17,25},{25,17},{2,10},{10... | collective-permute-start | bytes 9437192 | tf_op jit(solution)/shard_map/ppermute | solution.py:11
  221.7 98.7 %collective-permute-start.16 = (bf16[384,4096]{1,0:T(8,128)(2,1)S(1)}, bf16[384,4096]{1,0:T(8,128)(2,1)}, u32[]{:S(2)}, u32[]{:S(2)}) collective-permute-start(bf16[384,4096]{1,0:T(8,128)(2,1)S(1)} %fusion.18), channel_id=1, source_target_pairs={{0,16},{8,24},{16,0},{24,8},{1,17},{9,25},{17,1},{25,9},{2,18},{10... | collective-permute-start | bytes 9437192 | tf_op jit(solution)/shard_map/ppermute | solution.py:11
  333.4 71.0 %collective-permute-start.18 = (bf16[256,4096]{1,0:T(8,128)(2,1)}, bf16[256,4096]{1,0:T(8,128)(2,1)S(1)}, u32[]{:S(2)}, u32[]{:S(2)}) collective-permute-start(bf16[256,4096]{1,0:T(8,128)(2,1)} %collective-permute-done.10), channel_id=1, source_target_pairs={{2,0},{3,1},{10,8},{11,9},{18,16},{19,17},{26,24},{27,25}} | collective-permute-start | bytes 6291464 | tf_op jit(solution)/shard_map/ppermute | solution.py:25
  337.9 121.0 %collective-permute-start.23 = (bf16[256,4096]{1,0:T(8,128)(2,1)}, bf16[256,4096]{1,0:T(8,128)(2,1)}, u32[]{:S(2)}, u32[]{:S(2)}) collective-permute-start(bf16[256,4096]{1,0:T(8,128)(2,1)} %collective-permute-done.11), channel_id=1, source_target_pairs={{4,6},{5,7},{12,14},{13,15},{20,22},{21,23},{28,30},{29,31}} | collective-permute-start | bytes 6291464 | tf_op jit(solution)/shard_map/ppermute | solution.py:24
  364.0 94.9 %collective-permute-start.24 = (bf16[256,4096]{1,0:T(8,128)(2,1)}, bf16[256,4096]{1,0:T(8,128)(2,1)}, u32[]{:S(2)}, u32[]{:S(2)}) collective-permute-start(bf16[256,4096]{1,0:T(8,128)(2,1)} %collective-permute-done.12), channel_id=1, source_target_pairs={{2,0},{3,1},{10,8},{11,9},{18,16},{19,17},{26,24},{27,25}} | collective-permute-start | bytes 6291464 | tf_op jit(solution)/shard_map/ppermute | solution.py:25
  406.7 52.2 %collective-permute-start.21 = (bf16[256,4096]{1,0:T(8,128)(2,1)}, bf16[256,4096]{1,0:T(8,128)(2,1)}, u32[]{:S(2)}, u32[]{:S(2)}) collective-permute-start(bf16[256,4096]{1,0:T(8,128)(2,1)} %get-tuple-element.146), channel_id=1, source_target_pairs={{0,2},{1,3},{8,10},{9,11},{16,18},{17,19},{24,26},{25,27}} | collective-permute-start | bytes 6291464 | tf_op jit(solution)/shard_map/ppermute | solution.py:58
  409.6 49.3 %collective-permute-start.22 = (bf16[256,4096]{1,0:T(8,128)(2,1)}, bf16[256,4096]{1,0:T(8,128)(2,1)}, u32[]{:S(2)}, u32[]{:S(2)}) collective-permute-start(bf16[256,4096]{1,0:T(8,128)(2,1)} %get-tuple-element.145), channel_id=1, source_target_pairs={{6,4},{7,5},{14,12},{15,13},{22,20},{23,21},{30,28},{31,29}} | collective-permute-start | bytes 6291464 | tf_op jit(solution)/shard_map/ppermute | solution.py:59
  468.3 48.7 %collective-permute-start.31 = (bf16[192,4096]{1,0:T(8,128)(2,1)S(1)}, bf16[192,4096]{1,0:T(8,128)(2,1)}, u32[]{:S(2)}, u32[]{:S(2)}) collective-permute-start(bf16[192,4096]{1,0:T(8,128)(2,1)S(1)} %get-tuple-element.132), channel_id=1, source_target_pairs={{0,8},{8,0},{16,24},{24,16},{1,9},{9,1},{17,25},{25,17},{2,10},{10... | collective-permute-start | bytes 4718600 | tf_op jit(solution)/shard_map/ppermute | solution.py:11
  469.6 68.6 %collective-permute-start.32 = (bf16[192,4096]{1,0:T(8,128)(2,1)}, bf16[192,4096]{1,0:T(8,128)(2,1)}, u32[]{:S(2)}, u32[]{:S(2)}) collective-permute-start(bf16[192,4096]{1,0:T(8,128)(2,1)} %get-tuple-element.131), channel_id=1, source_target_pairs={{0,16},{8,24},{16,0},{24,8},{1,17},{9,25},{17,1},{25,9},{2,18},{10... | collective-permute-start | bytes 4718600 | tf_op jit(solution)/shard_map/ppermute | solution.py:11
  473.4 64.8 %collective-permute-start.27 = (bf16[256,4096]{1,0:T(8,128)(2,1)}, bf16[256,4096]{1,0:T(8,128)(2,1)}, u32[]{:S(2)}, u32[]{:S(2)}) collective-permute-start(bf16[256,4096]{1,0:T(8,128)(2,1)} %get-tuple-element.142), channel_id=1, source_target_pairs={{0,2},{1,3},{8,10},{9,11},{16,18},{17,19},{24,26},{25,27}} | collective-permute-start | bytes 6291464 | tf_op jit(solution)/shard_map/ppermute | solution.py:58
  554.1 58.5 %collective-permute-start.39 = (bf16[192,4096]{1,0:T(8,128)(2,1)S(1)}, bf16[192,4096]{1,0:T(8,128)(2,1)}, u32[]{:S(2)}, u32[]{:S(2)}) collective-permute-start(bf16[192,4096]{1,0:T(8,128)(2,1)S(1)} %get-tuple-element.128), channel_id=1, source_target_pairs={{0,8},{8,0},{16,24},{24,16},{1,9},{9,1},{17,25},{25,17},{2,10},{10... | collective-permute-start | bytes 4718600 | tf_op jit(solution)/shard_map/ppermute | solution.py:11
  555.4 63.2 %collective-permute-start.40 = (bf16[192,4096]{1,0:T(8,128)(2,1)S(1)}, bf16[192,4096]{1,0:T(8,128)(2,1)}, u32[]{:S(2)}, u32[]{:S(2)}) collective-permute-start(bf16[192,4096]{1,0:T(8,128)(2,1)S(1)} %get-tuple-element.127), channel_id=1, source_target_pairs={{0,16},{8,24},{16,0},{24,8},{1,17},{9,25},{17,1},{25,9},{2,18},{10... | collective-permute-start | bytes 4718600 | tf_op jit(solution)/shard_map/ppermute | solution.py:11
  556.8 72.6 %collective-permute-start.41 = (bf16[192,4096]{1,0:T(8,128)(2,1)S(1)}, bf16[192,4096]{1,0:T(8,128)(2,1)}, u32[]{:S(2)}, u32[]{:S(2)}) collective-permute-start(bf16[192,4096]{1,0:T(8,128)(2,1)S(1)} %get-tuple-element.126), channel_id=1, source_target_pairs={{0,8},{8,0},{16,24},{24,16},{1,9},{9,1},{17,25},{25,17},{2,10},{10... | collective-permute-start | bytes 4718600 | tf_op jit(solution)/shard_map/ppermute | solution.py:11
  586.3 79.5 %collective-permute-start.35 = (bf16[256,4096]{1,0:T(8,128)(2,1)}, bf16[256,4096]{1,0:T(8,128)(2,1)S(1)}, u32[]{:S(2)}, u32[]{:S(2)}) collective-permute-start(bf16[256,4096]{1,0:T(8,128)(2,1)} %get-tuple-element.138), channel_id=1, source_target_pairs={{0,2},{2,4},{1,3},{3,5},{8,10},{10,12},{9,11},{11,13},{16,18},{18,... | collective-permute-start | bytes 6291464 | tf_op jit(solution)/shard_map/ppermute | solution.py:58
  590.8 75.0 %collective-permute-start.36 = (bf16[256,4096]{1,0:T(8,128)(2,1)}, bf16[256,4096]{1,0:T(8,128)(2,1)}, u32[]{:S(2)}, u32[]{:S(2)}) collective-permute-start(bf16[256,4096]{1,0:T(8,128)(2,1)} %get-tuple-element.137), channel_id=1, source_target_pairs={{6,4},{4,2},{7,5},{5,3},{14,12},{12,10},{15,13},{13,11},{22,20},{2... | collective-permute-start | bytes 6291464 | tf_op jit(solution)/shard_map/ppermute | solution.py:59
  612.6 53.2 %collective-permute-start.33 = (bf16[256,4096]{1,0:T(8,128)(2,1)}, bf16[256,4096]{1,0:T(8,128)(2,1)}, u32[]{:S(2)}, u32[]{:S(2)}) collective-permute-start(bf16[256,4096]{1,0:T(8,128)(2,1)} %get-tuple-element.140), channel_id=1, source_target_pairs={{0,2},{2,4},{4,6},{1,3},{3,5},{5,7},{8,10},{10,12},{12,14},{9,11},... | collective-permute-start | bytes 6291464 | tf_op jit(solution)/shard_map/ppermute | solution.py:58
  (61 other events, 1834.4 us)

commit v2 on v1

--- a/solution.py
+++ b/solution.py
@@ -47,17 +47,23 @@
         start = jnp.clip(target, 0, size - 1) * rows
         return lax.dynamic_slice_in_dim(self.partial, start, rows, 0)
 
-    def step(self):
+    def blocks(self):
         size, at = lax.axis_size("ctx"), lax.axis_index("ctx")
         self.count += 1
         step = self.count
         up, down = self.block(at + size - step), self.block(at - size + step)
         if step > 1:
             up, down = up + self.arrived[0], down + self.arrived[1]
-        return [
-            lax.ppermute(up, "ctx", [(k, k + 1) for k in range(step)]),
-            lax.ppermute(down, "ctx", [(size - 1 - k, size - 2 - k) for k in range(step)]),
-        ]
+        return up, down
+
+    def push(self, value, step, way):
+        last = lax.axis_size("ctx") - 1
+        pairs = [(k, k + 1) if way > 0 else (last - k, last - 1 - k) for k in range(step)]
+        return lax.ppermute(value, "ctx", pairs)
+
+    def step(self):
+        up, down = self.blocks()
+        return [self.push(up, self.count, 1), self.push(down, self.count, -1)]
 
     def keep(self, arrived):
         self.arrived = arrived
@@ -70,25 +76,51 @@
         )
 
 
-def send_first(partial):
+def first_parts(partial):
     rows = partial.shape[0] // 4
     half = rows // 2
     for_x, for_y, across = [partial[k * rows : (k + 1) * rows] for k in (1, 2, 3)]
-    return [
-        swap(across[:half], 1),
-        swap(across[half:], 2),
-        swap(for_x[:half], 1),
-        swap(for_y[half:], 2),
-    ]
-
-
-def send_second(partial, first):
+    return (
+        jnp.concatenate([across[:half], for_x[:half]]),
+        jnp.concatenate([across[half:], for_y[half:]]),
+    )
+
+
+def second_parts(partial, first):
     rows = partial.shape[0] // 4
     half = rows // 2
-    return [
-        swap(partial[rows + half : 2 * rows] + first[1], 1),
-        swap(partial[2 * rows : 2 * rows + half] + first[0], 2),
-    ]
+    return (
+        partial[rows + half : 2 * rows] + first[1][:half],
+        partial[2 * rows : 2 * rows + half] + first[0][:half],
+    )
+
+
+def swap_both(parts):
+    return [swap(parts[0], 1), swap(parts[1], 2)]
+
+
+def send_first(partial):
+    return swap_both(first_parts(partial))
+
+
+def send_second(partial, first):
+    return swap_both(second_parts(partial, first))
+
+
+def both_sends(old, old_first, new):
+    half = old.shape[0] // 8
+    second, first = second_parts(old, old_first), first_parts(new)
+    sent = swap_both([jnp.concatenate([one, two]) for one, two in zip(second, first)])
+    return [one[:half] for one in sent], [one[half:] for one in sent]
+
+
+def both_steps(older, newer):
+    (up, down), (next_up, next_down) = older.blocks(), newer.blocks()
+    rows = up.shape[0]
+    step = older.count
+    up = older.push(jnp.concatenate([up, next_up]), step, 1)
+    down = older.push(jnp.concatenate([down, next_down]), step, -1)
+    return [up[:rows], down[:rows]], [up[rows:], down[rows:]]
 
 
 def sum_plane(partial, first, second):
@@ -96,8 +128,8 @@
     half = rows // 2
     return jnp.concatenate(
         [
-            wide(partial[:half]) + wide(first[2]) + wide(second[1]),
-            wide(partial[half:rows]) + wide(second[0]) + wide(first[3]),
+            wide(partial[:half]) + wide(first[0][half:]) + wide(second[1]),
+            wide(partial[half:rows]) + wide(second[0]) + wide(first[1][half:]),
         ]
     )
 
@@ -120,7 +152,7 @@
         return (gate * jax.nn.sigmoid(gate) * wide(up_pre[:, cut])).astype(jnp.bfloat16)
 
     def weight_dot(gathered):
-        return jnp.dot(turned, gathered.whole(), preferred_element_type=jnp.float32).astype(
+        return jnp.dot(turned, gathered, preferred_element_type=jnp.float32).astype(
             jnp.bfloat16
         )
 
@@ -140,20 +172,19 @@
             (grad_hidden * (gate * s)).astype(jnp.bfloat16),
         )
 
-    g0, g1 = Gather(w_down[:, cuts[0]]), Gather(w_down[:, cuts[1]])
+    gathered = Gather(w_down)
     h0 = activation(cuts[0])
-    a, b, c, x0, h1 = together(
+    a, x0, far, h1 = together(
         (
-            g0.step(),
-            g1.step(),
-            [features(0)] + [swap(features(k), k) for k in (1, 2, 3)],
-            [swap(h0, 1), swap(h0, 2)],
+            gathered.step(),
+            [swap(jnp.concatenate([h0, features(k)], axis=1), k) for k in (1, 2)],
+            swap(features(3), 3),
             activation(cuts[1]),
         )
     )
-    g0.keep(a)
-    g1.keep(b)
-    block = jnp.concatenate(c)
+    gathered.keep(a)
+    block = jnp.concatenate([features(0), x0[0][:, width:], x0[1][:, width:], far])
+    x0 = [x0[0][:, :width], x0[1][:, :width]]
     turned = jnp.concatenate(
         [
             lax.dynamic_slice_in_dim(block, lax.rem(at - j + size, size) * small, small, 1)
@@ -161,35 +192,37 @@
         ],
         axis=1,
     )
-    a, b, y0, x1 = together(
+    a, x1 = together(
         (
-            g0.step(),
-            g1.step(),
-            [swap(x0[1][:half], 1), swap(x0[0][half:], 2)],
-            [swap(h1, 1), swap(h1, 2)],
-        )
-    )
-    g0.keep(a)
-    g1.keep(b)
-    a, y1, d0 = together(
+            gathered.step(),
+            [
+                swap(jnp.concatenate([x0[1][:half], h1]), 1),
+                swap(jnp.concatenate([x0[0][half:], h1]), 2),
+            ],
+        )
+    )
+    gathered.keep(a)
+    y0 = [x1[0][:half], x1[1][:half]]
+    x1 = [x1[0][half:], x1[1][half:]]
+    s0 = Scatter(down_dot([h0] + x0 + y0))
+    a, y1, b = together(
         (
-            g0.step(),
+            gathered.step(),
             [swap(x1[1][:half], 1), swap(x1[0][half:], 2)],
-            down_dot([h0] + x0 + y0),
-        )
-    )
-    g0.keep(a)
-    s0 = Scatter(d0)
-    a, b, p0, d1 = together(
-        (s0.step(), g1.step(), weight_dot(g0), down_dot([h1] + x1 + y1))
-    )
-    s0.keep(a)
-    g1.keep(b)
-    s1 = Scatter(d1)
-    a, b, f0, p1 = together((s0.step(), s1.step(), send_first(p0), weight_dot(g1)))
+            s0.step(),
+        )
+    )
+    gathered.keep(a)
+    s0.keep(b)
+    weights = gathered.whole()
+    p0 = weight_dot(weights[:, cuts[0]])
+    s1 = Scatter(down_dot([h1] + x1 + y1))
+    a, b, f0, p1 = together(
+        (s0.step(), s1.step(), send_first(p0), weight_dot(weights[:, cuts[1]]))
+    )
     s0.keep(a)
     s1.keep(b)
-    a, b, e0, f1 = together((s0.step(), s1.step(), send_second(p0, f0), send_first(p1)))
+    a, b, e0, f1 = together(both_steps(s0, s1) + both_sends(p0, f0, p1))
     s0.keep(a)
     s1.keep(b)
     a, e1, o0 = together(

time: 759 us -> 698 us (0.920)
  waiting for transfers between devices: 435 us -> 377 us
  starting transfers between devices: 88.9 us -> 62.2 us
  other arithmetic: 92.5 us -> 115 us
    ppermute x12 -> x10, waiting for transfers between devices: 28 us -> 129 us  [push(): return lax.ppermute(value, 'ctx', pairs)]
    ppermute x23 -> x13, waiting for transfers between devices: 249 us -> 169 us  [swap(): return lax.ppermute(value, 'dp', pairs)]
    ppermute x6 -> x3, waiting for transfers between devices: 158 us -> 79.2 us  [step(): lax.ppermute(self.down[-1], 'ctx', [(k, k - 1) for k in range(1, size - s...]
    concatenate x0 -> x10, other arithmetic: none -> 26.8 us  [the longest x1 7.09 us: whole(): jnp.concatenate([self.own] + [jnp.where(at >= j, self.up[j], self.down[si...]
    ppermute x23 -> x13, starting transfers between devices: 24.8 us -> 13.3 us  [swap(): return lax.ppermute(value, 'dp', pairs)]
    ppermute x12 -> x10, starting transfers between devices: 40.5 us -> 32.7 us  [push(): return lax.ppermute(value, 'ctx', pairs)]
    slice x5 -> x10, local copies, waits for them, and re-layouts: 21.3 us -> 25.7 us  [the longest x4 10.9 us: both_sends(): return ([one[:half] for one in sent], [one[half:] for one in sent])]
    unnamed x86 -> x88, local copies, waits for them, and re-layouts: 21.8 us -> 25.8 us
  transfers between devices with their start and end apart: 47 -> 29, of which waited for: 20 -> 16; matrix products, arithmetic and copies ran while one was open for 22% -> 24% of each run, Pallas kernels for 0% -> 0%
where the time goes in v2:
time: 698 us; the launch traced here: 692 us
  waiting for transfers between devices  377 us (54%)
  other arithmetic  115 us (16%)
  matrix products  71 us (10%)
  local copies, waits for them, and re-layouts  65.6 us (9%)
  starting transfers between devices  62.2 us (9%)
    ppermute x13, waiting for transfers between devices, swap(): return lax.ppermute(value, 'dp', pairs)  169 us
    ppermute x10, waiting for transfers between devices, push(): return lax.ppermute(value, 'ctx', pairs)  129 us
    ppermute x3, waiting for transfers between devices, step(): lax.ppermute(self.down[-1], 'ctx', [(k, k - 1) for k in range(1, size - s...  79.2 us
    dot_general x2, matrix products, weight_dot(): jnp.dot(turned, gathered, preferred_element_type=jnp.float32)  37.8 us
    dot_general x2, matrix products, down_dot(): lax.dot_general(block, jnp.concatenate(parts), (((0,), (0,)), ((), ())),...  33.2 us
    ppermute x10, starting transfers between devices, push(): return lax.ppermute(value, 'ctx', pairs)  32.7 us
    unnamed x88, local copies, waits for them, and re-layouts  25.8 us
    add x4, other arithmetic, blocks(): up, down = (up + self.arrived[0], down + self.arrived[1])  18 us
  transfers between devices with their start and end apart: 29, of which 16 were waited for; matrix products, arithmetic and copies ran while one was open for 24% of the time, Pallas kernels for 0%

profile of v2, /device:TPU:0, one launch (start us, length us, event | category | flops | bytes accessed | tf_op | source)
XLA Modules:
  0.0 692.4 jit_solution(3798568007111180259)
XLA Ops:
  0.6 6.9 collective-permute-start
  21.9 98.8 %collective-permute-done.4 = bf16[384,1024]{1,0:T(8,128)(2,1)S(1)} collective-permute-done((bf16[384,1024]{1,0:T(8,128)(2,1)S(1)}, bf16[384,1024]{1,0:T(8,128)(2,1)S(1)}, u32[]{:S(2)}, u32[]{:S(2)}) %collective-permute-start.4) | collective-permute-done | bytes 786464 | tf_op jit(solution)/shard_map/ppermute | solution.py:11
  148.3 79.2 %collective-permute-done.6 = bf16[256,8192]{1,0:T(8,128)(2,1)} collective-permute-done((bf16[256,8192]{1,0:T(8,128)(2,1)}, bf16[256,8192]{1,0:T(8,128)(2,1)}, u32[]{:S(2)}, u32[]{:S(2)}) %collective-permute-start.6) | collective-permute-done | bytes 4194336 | tf_op jit(solution)/shard_map/ppermute | solution.py:25
  243.6 16.4 %convolution_convert_fusion.3 = bf16[1024,4096]{1,0:T(8,128)(2,1)S(1)} fusion(bf16[1536,4096]{1,0:T(8,128)(2,1)} %get-tuple-element.111, bf16[384,1024]{1,0:T(8,128)(2,1)S(1)} %copy-done.23, bf16[384,1024]{1,0:T(8,128)(2,1)S(1)} %slice.177, bf16[384,1024]{1,0:T(8,128)(2,1)S(1)} %slice.176, bf16[384,1024]{1,0:T(8,128)(2,1)S(1)} %copy-done.17), kind=kOutput, calls=%fused_computation.16 | convolution fusion | flops 12901679104 | bytes 24117248 | tf_op jit(solution)/shard_map/dot_general | solution.py:160
  267.5 26.0 %collective-permute-done.11 = bf16[192,4096]{1,0:T(8,128)(2,1)S(1)} collective-permute-done((bf16[192,4096]{1,0:T(8,128)(2,1)S(1)}, bf16[192,4096]{1,0:T(8,128)(2,1)S(1)}, u32[]{:S(2)}, u32[]{:S(2)}) %collective-permute-start.11) | collective-permute-done | bytes 1572896 | tf_op jit(solution)/shard_map/ppermute | solution.py:11
  293.5 6.6 collective-permute-start.13
  308.0 32.9 %collective-permute-done.13 = bf16[256,4096]{1,0:T(8,128)(2,1)S(1)} collective-permute-done((bf16[256,4096]{1,0:T(8,128)(2,1)S(1)}, bf16[256,4096]{1,0:T(8,128)(2,1)S(1)}, u32[]{:S(2)}, u32[]{:S(2)}) %collective-permute-start.13) | collective-permute-done | bytes 2097184 | tf_op jit(solution)/shard_map/ppermute | solution.py:62
  345.5 16.8 %convolution_convert_fusion.2 = bf16[1024,4096]{1,0:T(8,128)(2,1)S(1)} fusion(bf16[1536,4096]{1,0:T(8,128)(2,1)} %constant_dynamic-update-slice_fusion.1, bf16[384,1024]{1,0:T(8,128)(2,1)} %copy-done.22, bf16[384,1024]{1,0:T(8,128)(2,1)S(1)} %copy-done.15, bf16[384,1024]{1,0:T(8,128)(2,1)S(1)} %copy-done.13, bf16[384,1024]{1,0:T(8,128)(2,1)} %get-tuple-element.123), kind=kOutput, calls=%fused_computation.15 | convolution fusion | flops 12901679104 | bytes 24117248 | tf_op jit(solution)/shard_map/dot_general | solution.py:160
  368.9 6.1 collective-permute-start.17
  381.1 7.1 %pad_maximum_fusion = bf16[1024,8192]{1,0:T(8,128)(2,1)} fusion(bf16[256,8192]{1,0:T(8,128)(2,1)S(1)} %broadcast_select_fusion, bf16[256,8192]{1,0:T(8,128)(2,1)S(1)} %broadcast_select_fusion.1, bf16[256,8192]{1,0:T(8,128)(2,1)S(1)} %broadcast_select_fusion.2, bf16[256,8192]{1,0:T(8,128)(2,1)S(1)} %copy-done.11), kind=kLoop, calls=%fused_computation | loop fusion | flops 67108864 | bytes 33554432 | tf_op jit(solution)/shard_map/concatenate | solution.py:34
  388.2 18.9 %convolution_convert_fusion.1 = bf16[1536,4096]{1,0:T(8,128)(2,1)} fusion(bf16[1024,8192]{1,0:T(8,128)(2,1)} %pad_maximum_fusion, bf16[1536,256]{1,0:T(8,128)(2,1)} %get-tuple-element.121, bf16[1536,256]{1,0:T(8,128)(2,1)} %get-tuple-element.122, bf16[1536,256]{1,0:T(8,128)(2,1)S(1)} %copy-done.25, bf16[1536,256]{1,0:T(8,128)(2,1)S(1)} %copy-done.24), kind=kOutput, calls=%fused_computation.2 | convolution fusion | flops 12903776256 | bytes 24117248 | tf_op jit(solution)/shard_map/dot_general | solution.py:155
  423.9 18.9 %convolution_convert_fusion = bf16[1536,4096]{1,0:T(8,128)(2,1)} fusion(bf16[1024,8192]{1,0:T(8,128)(2,1)} %pad_maximum_fusion, bf16[1536,256]{1,0:T(8,128)(2,1)} %get-tuple-element.121, bf16[1536,256]{1,0:T(8,128)(2,1)} %get-tuple-element.122, bf16[1536,256]{1,0:T(8,128)(2,1)S(1)} %copy-done.25, bf16[1536,256]{1,0:T(8,128)(2,1)S(1)} %copy-done.24), kind=kOutput, calls=%fused_computation.1 | convolution fusion | flops 12903776256 | bytes 24117248 | tf_op jit(solution)/shard_map/dot_general | solution.py:155
  442.7 20.0 %collective-permute-done.15 = bf16[256,4096]{1,0:T(8,128)(2,1)} collective-permute-done((bf16[256,4096]{1,0:T(8,128)(2,1)}, bf16[256,4096]{1,0:T(8,128)(2,1)}, u32[]{:S(2)}, u32[]{:S(2)}) %collective-permute-start.15) | collective-permute-done | bytes 2097184 | tf_op jit(solution)/shard_map/ppermute | solution.py:62
  462.7 13.5 %collective-permute-done.19 = bf16[384,4096]{1,0:T(8,128)(2,1)} collective-permute-done((bf16[384,4096]{1,0:T(8,128)(2,1)S(1)}, bf16[384,4096]{1,0:T(8,128)(2,1)}, u32[]{:S(2)}, u32[]{:S(2)}) %collective-permute-start.19) | collective-permute-done | bytes 3145760 | tf_op jit(solution)/shard_map/ppermute | solution.py:11
  479.6 5.2 dynamic-slice_add_fusion.1
  484.9 5.4 dynamic-slice_add_fusion.2
  510.3 68.3 %collective-permute-done.21 = bf16[512,4096]{1,0:T(8,128)(2,1)} collective-permute-done((bf16[512,4096]{1,0:T(8,128)(2,1)}, bf16[512,4096]{1,0:T(8,128)(2,1)}, u32[]{:S(2)}, u32[]{:S(2)}) %collective-permute-start.21) | collective-permute-done | bytes 4194336 | tf_op jit(solution)/shard_map/ppermute | solution.py:62
  591.1 13.2 %collective-permute-done.23 = bf16[576,4096]{1,0:T(8,128)(2,1)} collective-permute-done((bf16[576,4096]{1,0:T(8,128)(2,1)}, bf16[576,4096]{1,0:T(8,128)(2,1)}, u32[]{:S(2)}, u32[]{:S(2)}) %collective-permute-start.23) | collective-permute-done | bytes 4718624 | tf_op jit(solution)/shard_map/ppermute | solution.py:11
  620.2 6.4 collective-permute-start.25
  631.9 8.3 %convert_add_fusion.3 = (f32[192,4096]{1,0:T(8,128)}, f32[192,4096]{1,0:T(8,128)}) fusion(bf16[192,4096]{1,0:T(8,128)(2,1)} %slice.235, bf16[1536,4096]{1,0:T(8,128)(2,1)} %convolution_convert_fusion.1, bf16[384,4096]{1,0:T(8,128)(2,1)} %collective-permute-done.19, bf16[384,4096]{1,0:T(8,128)(2,1)} %collective-permute-done.20, bf16[192,4096]{1,0:T(8,128)(2,1)} %slice.233), kind=kLoop, calls=%fused_computation.60 | loop fusion | flops 7864320 | bytes 15728640 | tf_op jit(solution)/shard_map/add | solution.py:131
  640.2 5.5 multiply_convert_fusion.3
  650.3 9.2 %collective-permute-done.28 = bf16[192,4096]{1,0:T(8,128)(2,1)} collective-permute-done((bf16[192,4096]{1,0:T(8,128)(2,1)}, bf16[192,4096]{1,0:T(8,128)(2,1)}, u32[]{:S(2)}, u32[]{:S(2)}) %collective-permute-start.28) | collective-permute-done | bytes 1572896 | tf_op jit(solution)/shard_map/ppermute | solution.py:11
  672.2 5.4 convert_add_fusion.1
  682.5 6.4 pad_maximum_fusion.4
  (181 shorter events, 189.6 us)
Async XLA Ops:
  0.6 120.2 %collective-permute-start = (bf16[256,8192]{1,0:T(8,128)(2,1)}, bf16[256,8192]{1,0:T(8,128)(2,1)}, u32[]{:S(2)}, u32[]{:S(2)}) collective-permute-start(bf16[256,8192]{1,0:T(8,128)(2,1)} %param.7), channel_id=1, source_target_pairs={{0,2},{2,4},{4,6},{1,3},{3,5},{5,7},{8,10},{10,12},{12,14},{9,11},... | collective-permute-start | bytes 12582920 | tf_op jit(solution)/shard_map/ppermute | solution.py:24
  7.5 113.3 %collective-permute-start.1 = (bf16[256,8192]{1,0:T(8,128)(2,1)}, bf16[256,8192]{1,0:T(8,128)(2,1)}, u32[]{:S(2)}, u32[]{:S(2)}) collective-permute-start(bf16[256,8192]{1,0:T(8,128)(2,1)} %param.7), channel_id=1, source_target_pairs={{2,0},{4,2},{6,4},{3,1},{5,3},{7,5},{10,8},{12,10},{14,12},{11,9},... | collective-permute-start | bytes 12582920 | tf_op jit(solution)/shard_map/ppermute | solution.py:25
  16.3 104.5 %collective-permute-start.3 = (bf16[384,5120]{1,0:T(8,128)(2,1)S(1)}, bf16[384,5120]{1,0:T(8,128)(2,1)S(1)}, u32[]{:S(2)}, u32[]{:S(2)}) collective-permute-start(bf16[384,5120]{1,0:T(8,128)(2,1)S(1)} %get-tuple-element.129), channel_id=1, source_target_pairs={{0,16},{8,24},{16,0},{24,8},{1,17},{9,25},{17,1},{25,9},{2,18},{10... | collective-permute-start | bytes 11796488 | tf_op jit(solution)/shard_map/ppermute | solution.py:11
  17.8 102.9 %collective-permute-start.2 = (bf16[384,5120]{1,0:T(8,128)(2,1)S(1)}, bf16[384,5120]{1,0:T(8,128)(2,1)S(1)}, u32[]{:S(2)}, u32[]{:S(2)}) collective-permute-start(bf16[384,5120]{1,0:T(8,128)(2,1)S(1)} %get-tuple-element.130), channel_id=1, source_target_pairs={{0,8},{8,0},{16,24},{24,16},{1,9},{9,1},{17,25},{25,17},{2,10},{10... | collective-permute-start | bytes 11796488 | tf_op jit(solution)/shard_map/ppermute | solution.py:11
  19.3 101.4 %collective-permute-start.4 = (bf16[384,1024]{1,0:T(8,128)(2,1)S(1)}, bf16[384,1024]{1,0:T(8,128)(2,1)S(1)}, u32[]{:S(2)}, u32[]{:S(2)}) collective-permute-start(bf16[384,1024]{1,0:T(8,128)(2,1)S(1)} %get-tuple-element.125), channel_id=1, source_target_pairs={{0,24},{8,16},{16,8},{24,0},{1,25},{9,17},{17,9},{25,1},{2,26},{10... | collective-permute-start | bytes 2359304 | tf_op jit(solution)/shard_map/ppermute | solution.py:11
  128.5 102.4 %collective-permute-start.8 = (bf16[576,4096]{1,0:T(8,128)(2,1)}, bf16[576,4096]{1,0:T(8,128)(2,1)}, u32[]{:S(2)}, u32[]{:S(2)}) collective-permute-start(bf16[576,4096]{1,0:T(8,128)(2,1)} %get-tuple-element.127), channel_id=1, source_target_pairs={{0,16},{8,24},{16,0},{24,8},{1,17},{9,25},{17,1},{25,9},{2,18},{10... | collective-permute-start | bytes 14155784 | tf_op jit(solution)/shard_map/ppermute | solution.py:11
  130.0 102.1 %collective-permute-start.7 = (bf16[576,4096]{1,0:T(8,128)(2,1)}, bf16[576,4096]{1,0:T(8,128)(2,1)}, u32[]{:S(2)}, u32[]{:S(2)}) collective-permute-start(bf16[576,4096]{1,0:T(8,128)(2,1)} %get-tuple-element.128), channel_id=1, source_target_pairs={{0,8},{8,0},{16,24},{24,16},{1,9},{9,1},{17,25},{25,17},{2,10},{10... | collective-permute-start | bytes 14155784 | tf_op jit(solution)/shard_map/ppermute | solution.py:11
  134.1 93.4 %collective-permute-start.6 = (bf16[256,8192]{1,0:T(8,128)(2,1)}, bf16[256,8192]{1,0:T(8,128)(2,1)}, u32[]{:S(2)}, u32[]{:S(2)}) collective-permute-start(bf16[256,8192]{1,0:T(8,128)(2,1)} %collective-permute-done.1), channel_id=1, source_target_pairs={{2,0},{4,2},{3,1},{5,3},{10,8},{12,10},{11,9},{13,11},{18,16},{20,... | collective-permute-start | bytes 12582920 | tf_op jit(solution)/shard_map/ppermute | solution.py:25
  232.1 108.8 %collective-permute-start.9 = (bf16[256,8192]{1,0:T(8,128)(2,1)}, bf16[256,8192]{1,0:T(8,128)(2,1)}, u32[]{:S(2)}, u32[]{:S(2)}) collective-permute-start(bf16[256,8192]{1,0:T(8,128)(2,1)} %collective-permute-done.5), channel_id=1, source_target_pairs={{4,6},{5,7},{12,14},{13,15},{20,22},{21,23},{28,30},{29,31}} | collective-permute-start | bytes 12582920 | tf_op jit(solution)/shard_map/ppermute | solution.py:24
  234.8 106.1 %collective-permute-start.10 = (bf16[256,8192]{1,0:T(8,128)(2,1)}, bf16[256,8192]{1,0:T(8,128)(2,1)}, u32[]{:S(2)}, u32[]{:S(2)}) collective-permute-start(bf16[256,8192]{1,0:T(8,128)(2,1)} %collective-permute-done.6), channel_id=1, source_target_pairs={{2,0},{3,1},{10,8},{11,9},{18,16},{19,17},{26,24},{27,25}} | collective-permute-start | bytes 12582920 | tf_op jit(solution)/shard_map/ppermute | solution.py:25
  261.6 46.4 %collective-permute-start.12 = (bf16[192,4096]{1,0:T(8,128)(2,1)}, bf16[192,4096]{1,0:T(8,128)(2,1)}, u32[]{:S(2)}, u32[]{:S(2)}) collective-permute-start(bf16[192,4096]{1,0:T(8,128)(2,1)} %get-tuple-element.114), channel_id=1, source_target_pairs={{0,16},{8,24},{16,0},{24,8},{1,17},{9,25},{17,1},{25,9},{2,18},{10... | collective-permute-start | bytes 4718600 | tf_op jit(solution)/shard_map/ppermute | solution.py:11
  264.1 43.9 %collective-permute-start.14 = (bf16[256,4096]{1,0:T(8,128)(2,1)}, bf16[256,4096]{1,0:T(8,128)(2,1)S(1)}, u32[]{:S(2)}, u32[]{:S(2)}) collective-permute-start(bf16[256,4096]{1,0:T(8,128)(2,1)} %get-tuple-element.109), channel_id=1, source_target_pairs={{6,4},{7,5},{14,12},{15,13},{22,20},{23,21},{30,28},{31,29}} | collective-permute-start | bytes 6291464 | tf_op jit(solution)/shard_map/ppermute | solution.py:62
  293.5 47.3 %collective-permute-start.13 = (bf16[256,4096]{1,0:T(8,128)(2,1)S(1)}, bf16[256,4096]{1,0:T(8,128)(2,1)S(1)}, u32[]{:S(2)}, u32[]{:S(2)}) collective-permute-start(bf16[256,4096]{1,0:T(8,128)(2,1)S(1)} %get-tuple-element.110), channel_id=1, source_target_pairs={{0,2},{1,3},{8,10},{9,11},{16,18},{17,19},{24,26},{25,27}} | collective-permute-start | bytes 6291464 | tf_op jit(solution)/shard_map/ppermute | solution.py:62
  366.9 54.2 %collective-permute-start.18 = (bf16[256,4096]{1,0:T(8,128)(2,1)}, bf16[256,4096]{1,0:T(8,128)(2,1)}, u32[]{:S(2)}, u32[]{:S(2)}) collective-permute-start(bf16[256,4096]{1,0:T(8,128)(2,1)} %get-tuple-element.105), channel_id=1, source_target_pairs={{6,4},{7,5},{14,12},{15,13},{22,20},{23,21},{30,28},{31,29}} | collective-permute-start | bytes 6291464 | tf_op jit(solution)/shard_map/ppermute | solution.py:62
  368.9 73.8 %collective-permute-start.17 = (bf16[256,4096]{1,0:T(8,128)(2,1)}, bf16[256,4096]{1,0:T(8,128)(2,1)}, u32[]{:S(2)}, u32[]{:S(2)}) collective-permute-start(bf16[256,4096]{1,0:T(8,128)(2,1)} %get-tuple-element.106), channel_id=1, source_target_pairs={{0,2},{1,3},{8,10},{9,11},{16,18},{17,19},{24,26},{25,27}} | collective-permute-start | bytes 6291464 | tf_op jit(solution)/shard_map/ppermute | solution.py:62
  411.2 65.0 %collective-permute-start.19 = (bf16[384,4096]{1,0:T(8,128)(2,1)S(1)}, bf16[384,4096]{1,0:T(8,128)(2,1)}, u32[]{:S(2)}, u32[]{:S(2)}) collective-permute-start(bf16[384,4096]{1,0:T(8,128)(2,1)S(1)} %pad_maximum_fusion.16), channel_id=1, source_target_pairs={{0,8},{8,0},{16,24},{24,16},{1,9},{9,1},{17,25},{25,17},{2,10},{10... | collective-permute-start | bytes 9437192 | tf_op jit(solution)/shard_map/ppermute | solution.py:11
  414.7 64.9 %collective-permute-start.20 = (bf16[384,4096]{1,0:T(8,128)(2,1)}, bf16[384,4096]{1,0:T(8,128)(2,1)}, u32[]{:S(2)}, u32[]{:S(2)}) collective-permute-start(bf16[384,4096]{1,0:T(8,128)(2,1)} %pad_maximum_fusion.17), channel_id=1, source_target_pairs={{0,16},{8,24},{16,0},{24,8},{1,17},{9,25},{17,1},{25,9},{2,18},{10... | collective-permute-start | bytes 9437192 | tf_op jit(solution)/shard_map/ppermute | solution.py:11
  421.1 41.7 %collective-permute-start.15 = (bf16[256,4096]{1,0:T(8,128)(2,1)}, bf16[256,4096]{1,0:T(8,128)(2,1)}, u32[]{:S(2)}, u32[]{:S(2)}) collective-permute-start(bf16[256,4096]{1,0:T(8,128)(2,1)} %get-tuple-element.108), channel_id=1, source_target_pairs={{0,2},{2,4},{1,3},{3,5},{8,10},{10,12},{9,11},{11,13},{16,18},{18,... | collective-permute-start | bytes 6291464 | tf_op jit(solution)/shard_map/ppermute | solution.py:62
  492.9 85.6 %collective-permute-start.21 = (bf16[512,4096]{1,0:T(8,128)(2,1)}, bf16[512,4096]{1,0:T(8,128)(2,1)}, u32[]{:S(2)}, u32[]{:S(2)}) collective-permute-start(bf16[512,4096]{1,0:T(8,128)(2,1)} %pad_maximum_fusion.9), channel_id=1, source_target_pairs={{0,2},{2,4},{4,6},{1,3},{3,5},{5,7},{8,10},{10,12},{12,14},{9,11},... | collective-permute-start | bytes 12582920 | tf_op jit(solution)/shard_map/ppermute | solution.py:62
  498.9 88.3 %collective-permute-start.22 = (bf16[512,4096]{1,0:T(8,128)(2,1)}, bf16[512,4096]{1,0:T(8,128)(2,1)}, u32[]{:S(2)}, u32[]{:S(2)}) collective-permute-start(bf16[512,4096]{1,0:T(8,128)(2,1)} %pad_maximum_fusion.10), channel_id=1, source_target_pairs={{6,4},{4,2},{2,0},{7,5},{5,3},{3,1},{14,12},{12,10},{10,8},{15,13}... | collective-permute-start | bytes 12582920 | tf_op jit(solution)/shard_map/ppermute | solution.py:62
  506.6 97.7 %collective-permute-start.23 = (bf16[576,4096]{1,0:T(8,128)(2,1)}, bf16[576,4096]{1,0:T(8,128)(2,1)}, u32[]{:S(2)}, u32[]{:S(2)}) collective-permute-start(bf16[576,4096]{1,0:T(8,128)(2,1)} %pad_maximum_fusion.7), channel_id=1, source_target_pairs={{0,8},{8,0},{16,24},{24,16},{1,9},{9,1},{17,25},{25,17},{2,10},{10... | collective-permute-start | bytes 14155784 | tf_op jit(solution)/shard_map/ppermute | solution.py:11
  509.6 99.7 %collective-permute-start.24 = (bf16[576,4096]{1,0:T(8,128)(2,1)}, bf16[576,4096]{1,0:T(8,128)(2,1)}, u32[]{:S(2)}, u32[]{:S(2)}) collective-permute-start(bf16[576,4096]{1,0:T(8,128)(2,1)} %pad_maximum_fusion.8), channel_id=1, source_target_pairs={{0,16},{8,24},{16,0},{24,8},{1,17},{9,25},{17,1},{25,9},{2,18},{10... | collective-permute-start | bytes 14155784 | tf_op jit(solution)/shard_map/ppermute | solution.py:11
  618.9 42.8 %collective-permute-start.26 = (bf16[256,4096]{1,0:T(8,128)(2,1)}, bf16[256,4096]{1,0:T(8,128)(2,1)}, u32[]{:S(2)}, u32[]{:S(2)}) collective-permute-start(bf16[256,4096]{1,0:T(8,128)(2,1)} %get-tuple-element.99), channel_id=1, source_target_pairs={{6,4},{4,2},{2,0},{7,5},{5,3},{3,1},{14,12},{12,10},{10,8},{15,13}... | collective-permute-start | bytes 6291464 | tf_op jit(solution)/shard_map/ppermute | solution.py:62
  620.2 42.7 %collective-permute-start.25 = (bf16[256,4096]{1,0:T(8,128)(2,1)}, bf16[256,4096]{1,0:T(8,128)(2,1)}, u32[]{:S(2)}, u32[]{:S(2)}) collective-permute-start(bf16[256,4096]{1,0:T(8,128)(2,1)} %get-tuple-element.100), channel_id=1, source_target_pairs={{0,2},{2,4},{4,6},{1,3},{3,5},{5,7},{8,10},{10,12},{12,14},{9,11},... | collective-permute-start | bytes 6291464 | tf_op jit(solution)/shard_map/ppermute | solution.py:62
  (46 other events, 739.9 us)
